TPU v7x, 32 devices: a whole 2x2x4 slice. The times are simulated.
32 devices in a mesh: groups: 2 (over y), trade: 4 (over z), scen: 2 (over x), hz: 2 (over core).
Axes of the slice: x: 2, y: 2, z: 4, core: 2. Of those that a mesh axis runs over, the one named last changes fastest.
Arguments:
- shocks: float32 [512, 512], P(('scen', 'hz'), 'trade'), may hold values from -5 to 5
- node_class: int32 [512], replicated, may hold values from 0 to 4
- positions: bfloat16 [16, 32768], P(None, ('groups', 'trade')), parts along dimension 1, may hold values from 0 to 31
- deltas: bfloat16 [16, 32768], P(None, ('groups', 'trade')), parts along dimension 1, may hold values from -0.5 to 0.5
- gammas: bfloat16 [16, 32768], P(None, ('groups', 'trade')), parts along dimension 1, may hold values from -0.5 to 0.5
- notional: bfloat16 [32768], P(('groups', 'trade')), parts along dimension 0, may hold values from -0.59765625 to 0.59765625
- block_desk: int32 [256], P(('groups', 'trade')), parts along dimension 0, may hold values from -1 to 7, as said below
Outputs:
- desk_pnl: float32 [16, 5, 512], P(('groups', 'trade'), None, ('scen', 'hz')), parts along dimension 0
There are 2 independent parts, one for each index of `groups`. A program takes and returns all parts, laid end to end along the dimension named above; an argument that names none is the same for every part. Nothing has to cross between parts.
Inputs may be any that keep to these rules, and one draw needn't show every extreme that they name: `block_desk`: all 128 trades of a block belong to one desk; on each trade index the live blocks come first and the empty ones (-1) after them; some trade index has all 32 blocks live; summed over the trade indices, the live blocks above 24 on an index never outnumber the places left below 24 on the others.
All inputs are finite; a program needn't handle non-finite values.
Results may differ from a plain program's by a relative error of at most 0.0055.
Values may be sent and summed in bfloat16 or wider, within the bound.
A program may use at most 64 MiB of HBM per device.

v0:
```python
import jax
import jax.numpy as jnp
from jax import lax
from jax.sharding import PartitionSpec as P

NODES = 512
BIN = 32
H = 5
BLK = 128
SLOTS = 32
HOLD = 24
DESK_DEV = 2


def tables(shocks, node_class):
    horizon_mask = (node_class[None, :] >= jnp.arange(H, dtype=jnp.int32)[:, None]).astype(
        jnp.float32
    )
    linear = (horizon_mask[:, None, :] * shocks[None, :, :]).astype(jnp.bfloat16)
    square = (0.5 * horizon_mask[:, None, :] * (shocks * shocks)[None, :, :]).astype(jnp.bfloat16)
    return (linear.reshape(-1, shocks.shape[1]), square.reshape(-1, shocks.shape[1]))


def group_pnl(linear, square, places, delta_rows, gamma_rows, values, desk_ids, desk_total):
    node_grid = jnp.arange(BIN, dtype=jnp.float32)[None, :, None]
    weights = jnp.maximum(0.0, 1.0 - jnp.abs(node_grid - places.astype(jnp.float32)[:, None, :]))
    delta_grid = (
        (delta_rows.astype(jnp.float32)[:, None, :] * weights)
        .astype(jnp.bfloat16)
        .reshape(NODES, -1)
    )
    gamma_grid = (
        (gamma_rows.astype(jnp.float32)[:, None, :] * weights)
        .astype(jnp.bfloat16)
        .reshape(NODES, -1)
    )
    response = jnp.dot(linear, delta_grid, preferred_element_type=jnp.float32)
    response = response + jnp.dot(square, gamma_grid, preferred_element_type=jnp.float32)
    profit = values.astype(jnp.float32)[None, :] * jnp.expm1(response)
    block_sums = jnp.sum(profit.reshape(profit.shape[0], desk_ids.shape[0], -1), axis=2)
    onehot = (desk_ids[None, :] == jnp.arange(desk_total, dtype=jnp.int32)[:, None]).astype(
        jnp.float32
    )
    return jnp.einsum("db,cb->dc", onehot, block_sums, precision=lax.Precision.HIGHEST)


def revalue(linear, square, places, delta_rows, gamma_rows, values, desk_ids, desk_total):
    group_blocks = SLOTS // 8
    group_rows = group_blocks * BLK
    group_count = desk_ids.shape[0] // group_blocks
    pillars = places.shape[0]

    def split_rows(array):
        return jnp.moveaxis(array.reshape(pillars, group_count, group_rows), 1, 0)

    stacked = (
        split_rows(places),
        split_rows(delta_rows),
        split_rows(gamma_rows),
        values.reshape(group_count, group_rows),
        desk_ids.reshape(group_count, group_blocks),
    )

    def accumulate(running, pieces):
        term = group_pnl(
            linear, square, pieces[0], pieces[1], pieces[2], pieces[3], pieces[4], desk_total
        )
        return (running + term, None)

    running, unused = lax.scan(
        accumulate, jnp.zeros((desk_total, linear.shape[0]), jnp.float32), stacked
    )
    return running


def assemble(own_rows, pooled_rows, picked):
    pillars = own_rows.shape[0]
    own_blocks = own_rows.reshape(pillars, SLOTS, BLK)[:, :HOLD]
    extra_blocks = pooled_rows.reshape(pillars, -1, BLK)
    joined = jnp.concatenate([own_blocks, extra_blocks], axis=1)
    return jnp.take(joined, picked, axis=1).reshape(pillars, HOLD * BLK)


def ledger(load_counts):
    surplus = jnp.maximum(load_counts - HOLD, 0)
    free_room = HOLD - jnp.minimum(load_counts, HOLD)
    first_surplus = jnp.cumsum(surplus) - surplus
    first_room = jnp.cumsum(free_room) - free_room
    return (surplus, free_room, first_surplus, first_room)


def place_pooled(
    linear, square, positions, deltas, gammas, notional, block_desk, load_counts, pooled, desk_total
):
    pooled_places, pooled_deltas, pooled_gammas, pooled_values, pooled_desks = pooled
    send_blocks = SLOTS - HOLD
    own_index = lax.axis_index("trade")
    surplus, free_room, first_surplus, first_room = ledger(load_counts)
    live_count = jnp.sum((block_desk >= 0).astype(jnp.int32))
    kept_count = jnp.minimum(live_count, HOLD)
    slot_ids = jnp.arange(HOLD, dtype=jnp.int32)
    wanted = first_room[own_index] + slot_ids - kept_count
    extra_ids = jnp.arange(send_blocks, dtype=jnp.int32)
    rank_ids = (first_surplus[:, None] + extra_ids[None, :]).reshape(-1)
    usable_pool = (extra_ids[None, :] < surplus[:, None]).reshape(-1)
    matches = (
        usable_pool[None, :]
        & (rank_ids[None, :] == wanted[:, None])
        & (slot_ids >= kept_count)[:, None]
    )
    found_any = jnp.any(matches, axis=1)
    source = jnp.sum(
        jnp.where(matches, jnp.arange(matches.shape[1], dtype=jnp.int32)[None, :], 0), axis=1
    )
    picked = jnp.where(slot_ids < kept_count, slot_ids, HOLD + source)
    usable_slot = (slot_ids < kept_count) | found_any
    places = assemble(positions, pooled_places, picked)
    delta_rows = assemble(deltas, pooled_deltas, picked)
    gamma_rows = assemble(gammas, pooled_gammas, picked)
    values = assemble(notional.reshape(1, -1), pooled_values, picked).reshape(-1)
    joined_desks = jnp.concatenate([block_desk[:HOLD], pooled_desks.reshape(-1)])
    desk_ids = jnp.where(usable_slot, jnp.take(joined_desks, picked), -1)
    return revalue(linear, square, places, delta_rows, gamma_rows, values, desk_ids, desk_total)


def body(shocks, node_class, positions, deltas, gammas, notional, block_desk):
    trade_count = lax.axis_size("trade")
    desk_total = DESK_DEV * trade_count
    all_nodes = lax.all_gather(shocks, "trade", axis=1, tiled=True)
    linear, square = tables(all_nodes, node_class)
    cut_rows = HOLD * BLK
    send_blocks = SLOTS - HOLD
    live_count = jnp.sum((block_desk >= 0).astype(jnp.int32)).reshape(1)
    load_counts = lax.all_gather(live_count, "trade", axis=0, tiled=True)
    surplus, free_room, first_surplus, first_room = ledger(load_counts)
    own_index = lax.axis_index("trade")
    extra_ids = jnp.arange(send_blocks, dtype=jnp.int32)
    global_rank = first_surplus[own_index] + extra_ids
    room_end = first_room + free_room
    target = jnp.sum((room_end[None, :] <= global_rank[:, None]).astype(jnp.int32), axis=1)
    valid = extra_ids < surplus[own_index]
    send_mask = valid[None, :] & (
        target[None, :] == jnp.arange(trade_count, dtype=jnp.int32)[:, None]
    )

    def spread(rows, fill):
        pillars = rows.shape[0]
        shaped = rows.reshape(pillars, 1, send_blocks, -1)
        placed = jnp.where(send_mask[None, :, :, None], shaped, jnp.asarray(fill, rows.dtype))
        return placed.reshape(pillars, -1)

    outgoing = (
        spread(positions[:, cut_rows:], 0),
        spread(deltas[:, cut_rows:], 0),
        spread(gammas[:, cut_rows:], 0),
        spread(notional[cut_rows:].reshape(1, -1), 0),
        spread(block_desk[HOLD:].reshape(1, -1), -1),
    )
    pooled = (
        lax.all_to_all(outgoing[0], "trade", split_axis=1, concat_axis=1, tiled=True),
        lax.all_to_all(outgoing[1], "trade", split_axis=1, concat_axis=1, tiled=True),
        lax.all_to_all(outgoing[2], "trade", split_axis=1, concat_axis=1, tiled=True),
        lax.all_to_all(outgoing[3], "trade", split_axis=1, concat_axis=1, tiled=True),
        lax.all_to_all(outgoing[4], "trade", split_axis=1, concat_axis=1, tiled=True),
    )
    partial_value = place_pooled(
        linear,
        square,
        positions,
        deltas,
        gammas,
        notional,
        block_desk,
        load_counts,
        pooled,
        desk_total,
    )
    owned = lax.psum_scatter(partial_value, "trade", scatter_dimension=0, tiled=True)
    return owned.reshape(owned.shape[0], H, -1)


def solution(mesh):
    in_specs = (
        P(("scen", "hz"), "trade"),
        P(),
        P(None, ("groups", "trade")),
        P(None, ("groups", "trade")),
        P(None, ("groups", "trade")),
        P(("groups", "trade")),
        P(("groups", "trade")),
    )
    out_specs = P(("groups", "trade"), None, ("scen", "hz"))
    return jax.shard_map(body, mesh=mesh, in_specs=in_specs, out_specs=out_specs, check_vma=False)
```

profile of v0, /device:TPU:0, one launch (start us, length us, event | category | flops | bytes accessed | tf_op | source)
XLA Modules:
  0.0 121.4 jit_solution(11088119055729940560)
XLA Ops:
  0.0 1.4 %fusion.18 = s32[]{:T(128)} fusion(s32[32]{0:T(128)} %param.17), kind=kLoop, calls=%fused_computation.70 | loop fusion | flops 95 | bytes 132 | tf_op jit(solution)/shard_map/reduce_sum | solution.py:133
  1.4 1.4 %fusion.23 = (u32[1]{0:T(128)}, u32[1]{0:T(128)}) fusion(u32[32]{0:T(128)} %constant.95, u32[]{:T(128)S(6)} %add.130, u32[]{:T(128)S(6)} %add.121), kind=kLoop, calls=%fused_computation.85 | loop fusion | bytes 24
  2.8 1.4 %dynamic-update-slice = s32[4]{0:T(128)S(1)} dynamic-update-slice(s32[4]{0:T(128)S(1)} %broadcast.376, s32[1]{0:T(128)} %bitcast, u32[]{:T(128)} %bitcast.1) | dynamic-update-slice | bytes 12
  5.0 10.0 %all-reduce = s32[4]{0:T(128)S(1)} all-reduce(s32[4]{0:T(128)S(1)} %dynamic-update-slice), channel_id=1, replica_groups=mesh['groups'=2,'trade'=4,'scen'=2,'hz'=2] {'trade'}, use_global_device_ids=true, to_apply=%add | all-reduce | flops 4 | bytes 32
  18.5 3.2 %all-to-all-start = ((s32[1,4,8]{2,0,1:T(1,128)}), s32[1,4,8]{2,0,1:T(1,128)S(1)}, u32[]{:S(2)}, u32[]{:S(2)}) async-start(s32[1,4,8]{2,0,1:T(1,128)} %and_select_fusion), calls=%async_computation | async-start | bytes 4096 | tf_op jit(solution)/shard_map/all_to_all | solution.py:164
  28.1 0.9 copy.79
  29.0 0.9 copy.81
  32.5 15.0 %all_gather.7 = f32[128,512]{1,0:T(8,128)S(1)} all-gather(f32[128,128]{1,0:T(8,128)S(1)} %copy-done.1), channel_id=1, replica_groups=mesh['groups'=2,'trade'=4,'scen'=2,'hz'=2] {'trade'}, dimensions={1}, use_global_device_ids=true | all-gather | bytes 327680 | tf_op jit(solution)/shard_map/all_gather | solution.py:129
  48.9 4.0 %all-to-all-start.1 = ((bf16[4,2,512]{2,1,0:T(2,128)(2,1)}), bf16[4,2,512]{2,1,0:T(2,128)(2,1)S(1)}, u32[]{:S(2)}, u32[]{:S(2)}) async-start(bf16[4,2,512]{2,1,0:T(2,128)(2,1)} %reshape.563), calls=%async_computation.1 | async-start | bytes 16384 | tf_op jit(solution)/shard_map/all_to_all | solution.py:163
  55.0 3.5 %all-to-all-done.1 = bf16[4,2,512]{2,1,0:T(2,128)(2,1)S(1)} async-done(((bf16[4,2,512]{2,1,0:T(2,128)(2,1)}), bf16[4,2,512]{2,1,0:T(2,128)(2,1)S(1)}, u32[]{:S(2)}, u32[]{:S(2)}) %all-to-all-start.1) | async-done | bytes 8224 | tf_op jit(solution)/shard_map/all_to_all | solution.py:163
  58.5 3.3 %all-to-all-start.2 = ((bf16[16,4,1024]{2,0,1:T(8,128)(2,1)}), bf16[16,4,1024]{2,0,1:T(8,128)(2,1)S(1)}, u32[]{:S(2)}, u32[]{:S(2)}) async-start(bf16[16,4,1024]{2,0,1:T(8,128)(2,1)} %get-tuple-element.185), calls=%async_computation.2 | async-start | bytes 262144 | tf_op jit(solution)/shard_map/all_to_all | solution.py:161
  62.5 5.2 %all-to-all-done.2 = bf16[16,4,1024]{2,0,1:T(8,128)(2,1)S(1)} async-done(((bf16[16,4,1024]{2,0,1:T(8,128)(2,1)}), bf16[16,4,1024]{2,0,1:T(8,128)(2,1)S(1)}, u32[]{:S(2)}, u32[]{:S(2)}) %all-to-all-start.2) | async-done | bytes 131104 | tf_op jit(solution)/shard_map/all_to_all | solution.py:161
  67.8 3.3 %all-to-all-start.3 = ((bf16[16,4,1024]{2,0,1:T(8,128)(2,1)}), bf16[16,4,1024]{2,0,1:T(8,128)(2,1)S(1)}, u32[]{:S(2)}, u32[]{:S(2)}) async-start(bf16[16,4,1024]{2,0,1:T(8,128)(2,1)} %get-tuple-element.184), calls=%async_computation.3 | async-start | bytes 262144 | tf_op jit(solution)/shard_map/all_to_all | solution.py:160
  71.3 6.2 %all-to-all-done.3 = bf16[16,4,1024]{2,0,1:T(8,128)(2,1)S(1)} async-done(((bf16[16,4,1024]{2,0,1:T(8,128)(2,1)}), bf16[16,4,1024]{2,0,1:T(8,128)(2,1)S(1)}, u32[]{:S(2)}, u32[]{:S(2)}) %all-to-all-start.3) | async-done | bytes 131104 | tf_op jit(solution)/shard_map/all_to_all | solution.py:160
  77.5 3.4 %all-to-all-start.4 = ((bf16[16,4,1024]{2,0,1:T(8,128)(2,1)}), bf16[16,4,1024]{2,0,1:T(8,128)(2,1)S(1)}, u32[]{:S(2)}, u32[]{:S(2)}) async-start(bf16[16,4,1024]{2,0,1:T(8,128)(2,1)} %get-tuple-element.183), calls=%async_computation.4 | async-start | bytes 262144 | tf_op jit(solution)/shard_map/all_to_all | solution.py:162
  82.4 4.5 %all-to-all-done.4 = bf16[16,4,1024]{2,0,1:T(8,128)(2,1)S(1)} async-done(((bf16[16,4,1024]{2,0,1:T(8,128)(2,1)}), bf16[16,4,1024]{2,0,1:T(8,128)(2,1)S(1)}, u32[]{:S(2)}, u32[]{:S(2)}) %all-to-all-start.4) | async-done | bytes 131104 | tf_op jit(solution)/shard_map/all_to_all | solution.py:162
  88.2 15.6 %while.11 = (s32[]{:T(128)}, f32[8,640]{1,0:T(8,128)S(1)}, s32[6,4]{1,0:T(8,128)S(1)}, bf16[6,512]{1,0:T(8,128)(2,1)S(1)}, bf16[6,16,512]{2,1,0:T(8,128)(2,1)S(1...) while((s32[]{:T(128)}, f32[8,640]{1,0:T(8,128)S(1)}, ...), condition=%wide.region_8.10_spmd.clone, body=%wide.region_6.9_spmd.clone.sunk | while | flops 675758080 | bytes 8205511 | solution.py:70
  89.6 1.1 bitcast_reduce_fusion.3
  92.2 1.1 bitcast_reduce_fusion.3
  94.8 1.1 bitcast_reduce_fusion.3
  97.4 1.1 bitcast_reduce_fusion.3
  100.0 1.1 bitcast_reduce_fusion.3
  102.6 1.1 bitcast_reduce_fusion.3
  103.9 17.0 %all-reduce.1 = f32[8,640]{1,0:T(8,128)S(1)} all-reduce(f32[8,640]{1,0:T(8,128)S(1)} %get-tuple-element.53), channel_id=2, replica_groups=mesh['groups'=2,'trade'=4,'scen'=2,'hz'=2] {'trade'}, use_global_device_ids=true, to_apply=%region_9.11.clone | all-reduce | flops 5120 | bytes 40960
  (168 shorter events, 28.3 us)
Async XLA Ops:
  0.0 30.0 %copy-start = (bf16[16,4096]{1,0:T(8,128)(2,1)S(1)}, bf16[16,4096]{1,0:T(8,128)(2,1)}, u32[]{:S(2)}) copy-start(bf16[16,4096]{1,0:T(8,128)(2,1)} %param.15) | copy-start | bytes 393220
  0.0 30.2 %slice-start = ((bf16[4096]{0:T(1024)(128)(2,1)}), bf16[1024]{0:T(1024)(128)(2,1)S(1)}, s32[]{:S(2)}) async-start(bf16[4096]{0:T(1024)(128)(2,1)} %param.16), calls=%async_computation.5 | async-start | bytes 4096 | tf_op jit(solution)/shard_map/slice | solution.py:156
  0.0 32.2 %copy-start.2 = (bf16[4096]{0:T(1024)(128)(2,1)S(1)}, bf16[4096]{0:T(1024)(128)(2,1)}, u32[]{:S(2)}) copy-start(bf16[4096]{0:T(1024)(128)(2,1)} %param.16) | copy-start | bytes 24580
  0.0 32.5 %copy-start.1 = (f32[128,128]{1,0:T(8,128)S(1)}, f32[128,128]{1,0:T(8,128)}, u32[]{:S(2)}) copy-start(f32[128,128]{1,0:T(8,128)} %param.11) | copy-start | bytes 196612
  18.5 30.4 %all-to-all-start = ((s32[1,4,8]{2,0,1:T(1,128)}), s32[1,4,8]{2,0,1:T(1,128)S(1)}, u32[]{:S(2)}, u32[]{:S(2)}) async-start(s32[1,4,8]{2,0,1:T(1,128)} %and_select_fusion), calls=%async_computation | async-start | bytes 4096 | tf_op jit(solution)/shard_map/all_to_all | solution.py:164
  30.0 24.2 %copy-start.3 = (s32[32]{0:T(128)S(1)}, s32[32]{0:T(128)}, u32[]{:S(2)}) copy-start(s32[32]{0:T(128)} %param.17) | copy-start | bytes 388
  48.9 9.6 %all-to-all-start.1 = ((bf16[4,2,512]{2,1,0:T(2,128)(2,1)}), bf16[4,2,512]{2,1,0:T(2,128)(2,1)S(1)}, u32[]{:S(2)}, u32[]{:S(2)}) async-start(bf16[4,2,512]{2,1,0:T(2,128)(2,1)} %reshape.563), calls=%async_computation.1 | async-start | bytes 16384 | tf_op jit(solution)/shard_map/all_to_all | solution.py:163
  58.5 9.3 %all-to-all-start.2 = ((bf16[16,4,1024]{2,0,1:T(8,128)(2,1)}), bf16[16,4,1024]{2,0,1:T(8,128)(2,1)S(1)}, u32[]{:S(2)}, u32[]{:S(2)}) async-start(bf16[16,4,1024]{2,0,1:T(8,128)(2,1)} %get-tuple-element.185), calls=%async_computation.2 | async-start | bytes 262144 | tf_op jit(solution)/shard_map/all_to_all | solution.py:161
  67.8 9.7 %all-to-all-start.3 = ((bf16[16,4,1024]{2,0,1:T(8,128)(2,1)}), bf16[16,4,1024]{2,0,1:T(8,128)(2,1)S(1)}, u32[]{:S(2)}, u32[]{:S(2)}) async-start(bf16[16,4,1024]{2,0,1:T(8,128)(2,1)} %get-tuple-element.184), calls=%async_computation.3 | async-start | bytes 262144 | tf_op jit(solution)/shard_map/all_to_all | solution.py:160
  77.5 9.3 %all-to-all-start.4 = ((bf16[16,4,1024]{2,0,1:T(8,128)(2,1)}), bf16[16,4,1024]{2,0,1:T(8,128)(2,1)S(1)}, u32[]{:S(2)}, u32[]{:S(2)}) async-start(bf16[16,4,1024]{2,0,1:T(8,128)(2,1)} %get-tuple-element.183), calls=%async_computation.4 | async-start | bytes 262144 | tf_op jit(solution)/shard_map/all_to_all | solution.py:162
where the time goes:
time: 122 us; the launch traced here: 121 us
  blocking collectives  41.9 us (34%)
  waiting for transfers between devices  19.3 us (16%)
  local copies, waits for them, and re-layouts  17.4 us (14%)
  starting transfers between devices  17.3 us (14%)
  other arithmetic  12.5 us (10%)
  matrix products  10.9 us (9%)
  between operations  1.8 us (1%)
    unnamed x2, blocking collectives  26.9 us
    all_gather x1, blocking collectives, body(): all_nodes = lax.all_gather(shocks, 'trade', axis=1, tiled=True)  15 us
    dot_general x6, matrix products, group_pnl(): jnp.dot(square, gamma_grid, preferred_element_type=jnp.float32)  6.43 us
    unnamed x25, local copies, waits for them, and re-layouts  6.18 us
    all_to_all x1, waiting for transfers between devices, body(): lax.all_to_all(outgoing[0], 'trade', split_axis=1, concat_axis=1, tiled=T...  6.17 us
    all_to_all x1, waiting for transfers between devices, body(): lax.all_to_all(outgoing[1], 'trade', split_axis=1, concat_axis=1, tiled=T...  5.22 us
    all_to_all x1, waiting for transfers between devices, body(): lax.all_to_all(outgoing[2], 'trade', split_axis=1, concat_axis=1, tiled=T...  4.46 us
    all_to_all x1, starting transfers between devices, body(): lax.all_to_all(outgoing[3], 'trade', split_axis=1, concat_axis=1, tiled=T...  3.98 us
  transfers between devices with their start and end apart: 5, of which 4 were waited for; matrix products, arithmetic and copies ran while one was open for 12% of the time, Pallas kernels for 0%

commit v1 on v0

v1 whole, which is shorter than its diff:
```python
import functools

import jax
import jax.numpy as jnp
from jax import lax
from jax.experimental import pallas as pl
from jax.experimental.pallas import tpu as pltpu
from jax.sharding import PartitionSpec as P

BIN = 32
H = 5
BLK = 128
CHUNK = 512
MESH = pl.DeviceIdType.MESH


def kernel(
    n, shocks_ref, class_ref, pos_ref, del_ref, gam_ref, val_ref, desk_ref, out_ref,
    held, table, grid, owner, total, parts, landed, send_a, recv_a, send_b, recv_b,
):
    me = lax.axis_index("trade")
    scens, cols = shocks_ref.shape
    pillars, trades = pos_ref.shape
    nodes = n * cols
    blocks = trades // BLK
    per_device = out_ref.shape[0]
    desk_rows = owner.shape[0]

    barrier = pltpu.get_barrier_semaphore()
    for off in range(1, n):
        pl.semaphore_signal(
            barrier, inc=1, device_id={"trade": lax.rem(me + off, n)}, device_id_type=MESH
        )

    own = shocks_ref[...]
    held[me, :scens, :] = own.astype(jnp.bfloat16)
    held[me, scens:, :] = (0.5 * (own * own)).astype(jnp.bfloat16)
    pl.semaphore_wait(barrier, n - 1)

    def gather_copy(slot, peer):
        return pltpu.make_async_remote_copy(
            src_ref=held.at[slot],
            dst_ref=held.at[slot],
            send_sem=send_a.at[peer],
            recv_sem=recv_a.at[slot],
            device_id={"trade": peer},
            device_id_type=MESH,
        )

    for off in range(1, n):
        gather_copy(me, lax.rem(me + off, n)).start()

    desk_iota = lax.broadcasted_iota(jnp.int32, (desk_rows, BLK), 0)

    def place_owner(b, carry):
        lanes = pl.ds(pl.multiple_of(b * BLK, BLK), BLK)
        row = val_ref[:, lanes].astype(jnp.float32)
        owner[:, lanes] = jnp.where(desk_iota == desk_ref[0, b], row, 0.0).astype(jnp.bfloat16)
        return carry

    lax.fori_loop(0, blocks, place_owner, 0)
    node_iota = lax.broadcasted_iota(jnp.int32, (BIN, CHUNK), 0).astype(jnp.float32)

    def build(c, carry):
        lanes = pl.ds(pl.multiple_of(c * CHUNK, CHUNK), CHUNK)
        pos = pos_ref[:, lanes].astype(jnp.float32)
        delta = del_ref[:, lanes].astype(jnp.float32)
        gamma = gam_ref[:, lanes].astype(jnp.float32)
        for p in range(pillars):
            weight = jnp.maximum(0.0, 1.0 - jnp.abs(node_iota - pos[p : p + 1, :]))
            grid[p * BIN : (p + 1) * BIN, lanes] = (delta[p : p + 1, :] * weight).astype(jnp.bfloat16)
            grid[nodes + p * BIN : nodes + (p + 1) * BIN, lanes] = (
                gamma[p : p + 1, :] * weight
            ).astype(jnp.bfloat16)
        return carry

    lax.fori_loop(0, trades // CHUNK, build, 0)

    for off in range(1, n):
        slot = lax.rem(me + n - off, n)
        gather_copy(slot, slot).wait_recv()
    for h in range(H):
        live = (class_ref[...] >= h).astype(jnp.float32).astype(jnp.bfloat16)
        line = jnp.concatenate([held[k, :scens, :] for k in range(n)], axis=1)
        table[h * scens : (h + 1) * scens, :nodes] = line * live
        line = jnp.concatenate([held[k, scens:, :] for k in range(n)], axis=1)
        table[h * scens : (h + 1) * scens, nodes:] = line * live

    total[...] = jnp.zeros_like(total)

    def value(c, carry):
        lanes = pl.ds(pl.multiple_of(c * CHUNK, CHUNK), CHUNK)
        response = jnp.dot(table[...], grid[:, lanes], preferred_element_type=jnp.float32)
        growth = (jnp.exp(response) - 1.0).astype(jnp.bfloat16)
        total[...] += lax.dot_general(
            owner[:, lanes], growth, (((1,), (1,)), ((), ())), preferred_element_type=jnp.float32
        )
        return carry

    lax.fori_loop(0, trades // CHUNK, value, 0)

    for k in range(n):
        for d in range(per_device):
            for h in range(H):
                parts[k, d, h : h + 1, :] = total[
                    k * per_device + d : k * per_device + d + 1, h * scens : (h + 1) * scens
                ]

    def share_copy(slot, peer):
        return pltpu.make_async_remote_copy(
            src_ref=parts.at[peer],
            dst_ref=landed.at[slot],
            send_sem=send_b.at[peer],
            recv_sem=recv_b.at[slot],
            device_id={"trade": peer},
            device_id_type=MESH,
        )

    for off in range(1, n):
        share_copy(me, lax.rem(me + off, n)).start()
    result = parts[me]
    for off in range(1, n):
        slot = lax.rem(me + n - off, n)
        share_copy(slot, slot).wait_recv()
        result = result + landed[slot]
    out_ref[...] = result[:, :H, :]
    for off in range(1, n):
        peer = lax.rem(me + off, n)
        gather_copy(me, peer).wait_send()
        share_copy(me, peer).wait_send()


def body(shocks, node_class, positions, deltas, gammas, notional, block_desk):
    n = lax.axis_size("trade")
    scens, cols = shocks.shape
    pillars, trades = positions.shape
    nodes = n * cols
    per_device = 2
    desk_rows = -(-(per_device * n) // 16) * 16
    vmem = pl.BlockSpec(memory_space=pltpu.VMEM)
    return pl.pallas_call(
        functools.partial(kernel, n),
        out_shape=jax.ShapeDtypeStruct((per_device, H, scens), jnp.float32),
        in_specs=[vmem] * 6 + [pl.BlockSpec(memory_space=pltpu.SMEM)],
        out_specs=vmem,
        scratch_shapes=[
            pltpu.VMEM((n, 2 * scens, cols), jnp.bfloat16),
            pltpu.VMEM((H * scens, 2 * nodes), jnp.bfloat16),
            pltpu.VMEM((2 * nodes, trades), jnp.bfloat16),
            pltpu.VMEM((desk_rows, trades), jnp.bfloat16),
            pltpu.VMEM((desk_rows, H * scens), jnp.float32),
            pltpu.VMEM((n, per_device, 8, scens), jnp.float32),
            pltpu.VMEM((n, per_device, 8, scens), jnp.float32),
            pltpu.SemaphoreType.DMA((n,)),
            pltpu.SemaphoreType.DMA((n,)),
            pltpu.SemaphoreType.DMA((n,)),
            pltpu.SemaphoreType.DMA((n,)),
        ],
        compiler_params=pltpu.CompilerParams(
            collective_id=0, has_side_effects=True, vmem_limit_bytes=40 * 1024 * 1024
        ),
    )(
        shocks,
        node_class.reshape(1, -1),
        positions,
        deltas,
        gammas,
        notional.reshape(1, -1),
        block_desk.reshape(1, -1),
    )


def solution(mesh):
    in_specs = (
        P(("scen", "hz"), "trade"),
        P(),
        P(None, ("groups", "trade")),
        P(None, ("groups", "trade")),
        P(None, ("groups", "trade")),
        P(("groups", "trade")),
        P(("groups", "trade")),
    )
    out_specs = P(("groups", "trade"), None, ("scen", "hz"))
    return jax.shard_map(body, mesh=mesh, in_specs=in_specs, out_specs=out_specs, check_vma=False)
```

time: 122 us -> 30 us (0.25)
  blocking collectives: 41.9 us -> 0 us
  Pallas kernels: 0 us -> 24.8 us
  waiting for transfers between devices: 19.3 us -> 0 us
  starting transfers between devices: 17.3 us -> 0 us
  local copies, waits for them, and re-layouts: 17.4 us -> 4.88 us
  other arithmetic: 12.5 us -> 0 us
  matrix products: 10.9 us -> 0 us
  between operations: 1.8 us -> 0.04 us
    unnamed x2 -> x0, blocking collectives: 26.9 us -> none
    pallas_call x0 -> x1, Pallas kernels: none -> 24.8 us  [body(): pl.pallas_call(functools.partial(kernel, n), out_shape=jax.ShapeDtypeStru...]
    all_to_all x5 -> x0, waiting for transfers between devices: 19.3 us -> none  [the longest x1 6.17 us: body(): lax.all_to_all(outgoing[0], 'trade', split_axis=1, concat_axis=1, tiled=T...]
    all_to_all x5 -> x0, starting transfers between devices: 17.3 us -> none  [the longest x1 3.98 us: body(): lax.all_to_all(outgoing[3], 'trade', split_axis=1, concat_axis=1, tiled=T...]
    all_gather x1 -> x0, blocking collectives: 15 us -> none  [body(): all_nodes = lax.all_gather(shocks, 'trade', axis=1, tiled=True)]
    dot_general x18 -> x0, matrix products: 10.9 us -> none  [the longest x6 6.43 us: group_pnl(): jnp.dot(square, gamma_grid, preferred_element_type=jnp.float32)]
    convert_element_type x25 -> x0, other arithmetic: 4.4 us -> none  [the longest x6 1.84 us: group_pnl(): gamma_grid = (gamma_rows.astype(jnp.float32)[:, None, :] * weights).astyp...]
    gather x7 -> x0, local copies, waits for them, and re-layouts: 3.13 us -> none  [the longest x5 2.35 us: assemble(): return jnp.take(joined, picked, axis=1).reshape(pillars, HOLD * BLK)]
  transfers between devices with their start and end apart: 5 -> 0, of which waited for: 4 -> 0; matrix products, arithmetic and copies ran while one was open for 12% -> 0% of each run, Pallas kernels for 0% -> 0%
where the time goes in v1:
time: 30 us; the launch traced here: 29.7 us
  Pallas kernels  24.8 us (83%)
  local copies, waits for them, and re-layouts  4.88 us (16%)
    pallas_call x1, Pallas kernels, body(): pl.pallas_call(functools.partial(kernel, n), out_shape=jax.ShapeDtypeStru...  24.8 us
    unnamed x12, local copies, waits for them, and re-layouts  3.55 us
    reshape x1, local copies, waits for them, and re-layouts, body(): notional.reshape(1, -1)  0.73 us

profile of v1, /device:TPU:0, one launch (start us, length us, event | category | flops | bytes accessed | tf_op | source)
XLA Modules:
  0.0 29.7 jit_solution(17584810461330497043)
XLA Ops:
  0.0 0.0 copy-start.4
  0.0 0.0 copy-start.5
  0.0 0.7 %reshape.10.val_ref = bf16[1,4096]{1,0:T(2,128)(2,1)S(1)} reshape(bf16[4096]{0:T(1024)(128)(2,1)} %param.12) | data formatting | bytes 16384 | tf_op jit(solution)/shard_map/reshape | solution.py:168
  0.7 0.0 copy-done.4
  0.8 0.0 copy-done.5
  0.8 0.0 copy-start
  0.8 0.9 %copy-done = bf16[16,4096]{1,0:T(8,128)(2,1)S(1)} copy-done((bf16[16,4096]{1,0:T(8,128)(2,1)S(1)}, bf16[16,4096]{1,0:T(8,128)(2,1)}, u32[]{:S(2)}) %copy-start) | copy-done | bytes 131096
  1.7 0.0 copy-start.1
  1.7 0.9 %copy-done.1 = bf16[16,4096]{1,0:T(8,128)(2,1)S(1)} copy-done((bf16[16,4096]{1,0:T(8,128)(2,1)S(1)}, bf16[16,4096]{1,0:T(8,128)(2,1)}, u32[]{:S(2)}) %copy-start.1) | copy-done | bytes 131096
  2.6 0.0 copy-start.2
  2.6 0.9 %copy-done.2 = bf16[16,4096]{1,0:T(8,128)(2,1)S(1)} copy-done((bf16[16,4096]{1,0:T(8,128)(2,1)S(1)}, bf16[16,4096]{1,0:T(8,128)(2,1)}, u32[]{:S(2)}) %copy-start.2) | copy-done | bytes 131096
  3.5 0.0 copy-start.3
  3.5 0.8 %copy-done.3 = f32[128,128]{1,0:T(8,128)S(1)} copy-done((f32[128,128]{1,0:T(8,128)S(1)}, f32[128,128]{1,0:T(8,128)}, u32[]{:S(2)}) %copy-start.3) | copy-done | bytes 65560
  4.3 24.8 %shard_map.73 = f32[2,5,128]{2,1,0:T(8,128)S(1)} custom-call(f32[128,128]{1,0:T(8,128)S(1)} %copy-done.3, s32[1,512]{1,0:T(1,128)S(1)} %bitcast.2, bf16[16,4096]{1,0:T(8,128)(2,1)S(1)} %copy-done, bf16[16,4096]{1,0:T(8,128)(2,1)S(1)} %copy-done.1, bf16[16,4096]{1,0:T(8,128)(2,1)S(1)} %copy-done.2, bf16[1,4096]{1,0:T(2,128)(2,1)S(1)} %reshape.10.val_ref, ...), custom_call_target="tpu_custom_call" | custom-call | tf_op jit(solution)/shard_map/pallas_call | solution.py:141
  29.1 0.6 %copy.8 = f32[2,5,128]{2,0,1:T(2,128)} copy(f32[2,5,128]{2,1,0:T(8,128)S(1)} %shard_map.73) | data formatting | bytes 10240 | tf_op jit(solution)/shard_map/pallas_call | solution.py:141
Async XLA Ops:
  0.0 0.7 %copy-start.4 = (s32[512]{0:T(512)S(1)}, s32[512]{0:T(512)}, u32[]{:S(2)}) copy-start(s32[512]{0:T(512)} %param.8) | copy-start | bytes 6148
  0.0 0.8 %copy-start.5 = (s32[32]{0:T(128)S(1)}, s32[32]{0:T(128)}, u32[]{:S(2)}) copy-start(s32[32]{0:T(128)} %param.13) | copy-start | bytes 388
  0.8 0.9 %copy-start = (bf16[16,4096]{1,0:T(8,128)(2,1)S(1)}, bf16[16,4096]{1,0:T(8,128)(2,1)}, u32[]{:S(2)}) copy-start(bf16[16,4096]{1,0:T(8,128)(2,1)} %pos_ref.1) | copy-start | bytes 393220
  1.7 0.9 %copy-start.1 = (bf16[16,4096]{1,0:T(8,128)(2,1)S(1)}, bf16[16,4096]{1,0:T(8,128)(2,1)}, u32[]{:S(2)}) copy-start(bf16[16,4096]{1,0:T(8,128)(2,1)} %del_ref.1) | copy-start | bytes 393220
  2.6 0.9 %copy-start.2 = (bf16[16,4096]{1,0:T(8,128)(2,1)S(1)}, bf16[16,4096]{1,0:T(8,128)(2,1)}, u32[]{:S(2)}) copy-start(bf16[16,4096]{1,0:T(8,128)(2,1)} %gam_ref.1) | copy-start | bytes 393220
  3.5 0.8 %copy-start.3 = (f32[128,128]{1,0:T(8,128)S(1)}, f32[128,128]{1,0:T(8,128)}, u32[]{:S(2)}) copy-start(f32[128,128]{1,0:T(8,128)} %shocks_ref.1) | copy-start | bytes 196612

commit v2 on v1

v2 whole, which is shorter than its diff:
```python
import functools

import jax
import jax.numpy as jnp
from jax import lax
from jax.experimental import pallas as pl
from jax.experimental.pallas import tpu as pltpu
from jax.sharding import PartitionSpec as P

BIN = 32
H = 5
BLK = 128
CHUNK = 1024
SUB = 256
VLIM = 60
MESH = pl.DeviceIdType.MESH


def kernel(
    n, shocks_hbm, class_ref, pos_hbm, del_hbm, gam_hbm, val_hbm, desk_ref, out_ref,
    shocks_ref, pos_ref, del_ref, gam_ref, val_ref, load_sem, held, table, grid, owner, total, even, odd, parts, landed, send_a, recv_a, send_b, recv_b, swap_sem,
):
    me = lax.axis_index("trade")
    side = lax.axis_index("groups")
    scens, cols = shocks_ref.shape
    pillars, trades = pos_ref.shape
    nodes = n * cols
    rows = scens // 2
    blocks = trades // BLK
    per_device = out_ref.shape[0]
    desk_rows = owner.shape[0]

    loads = [
        pltpu.make_async_copy(source, target, load_sem.at[i])
        for i, (source, target) in enumerate(
            [
                (shocks_hbm, shocks_ref),
                (val_hbm, val_ref),
                (pos_hbm, pos_ref),
                (del_hbm, del_ref),
                (gam_hbm, gam_ref),
            ]
        )
    ]
    for load in loads:
        load.start()
    barrier = pltpu.get_barrier_semaphore()
    for off in range(1, n):
        pl.semaphore_signal(
            barrier, inc=1, device_id={"trade": lax.rem(me + off, n)}, device_id_type=MESH
        )

    pl.semaphore_signal(
        barrier, inc=1, device_id={"groups": 1 - side}, device_id_type=MESH
    )
    loads[0].wait()
    own = shocks_ref[pl.ds(pl.multiple_of(side * rows, rows), rows), :]
    held[side, me, :rows, :] = own.astype(jnp.bfloat16)
    held[side, me, rows:, :] = (0.5 * (own * own)).astype(jnp.bfloat16)
    pl.semaphore_wait(barrier, n)

    def gather_copy(slot, peer):
        return pltpu.make_async_remote_copy(
            src_ref=held.at[side, slot],
            dst_ref=held.at[side, slot],
            send_sem=send_a.at[peer],
            recv_sem=recv_a.at[slot],
            device_id={"trade": peer},
            device_id_type=MESH,
        )

    def swap_copy(half):
        return pltpu.make_async_remote_copy(
            src_ref=held.at[half],
            dst_ref=held.at[half],
            send_sem=swap_sem.at[0],
            recv_sem=swap_sem.at[1],
            device_id={"groups": 1 - side},
            device_id_type=MESH,
        )

    for off in range(1, n):
        gather_copy(me, lax.rem(me + off, n)).start()

    for load in loads[1:]:
        load.wait()

    desk_iota = lax.broadcasted_iota(jnp.int32, (desk_rows, BLK), 0)

    values = val_ref[...].astype(jnp.float32).reshape(1, trades)
    for b in range(blocks):
        row = values[:, b * BLK : (b + 1) * BLK]
        owner[:, b * BLK : (b + 1) * BLK] = jnp.where(desk_iota == desk_ref[b], row, 0.0).astype(
            jnp.bfloat16
        )
    node_iota = lax.broadcasted_iota(jnp.int32, (BIN, CHUNK), 0).astype(jnp.float32)

    def build(c, carry):
        lanes = pl.ds(pl.multiple_of(c * CHUNK, CHUNK), CHUNK)
        pos = pos_ref[:, lanes].astype(jnp.float32)
        delta = del_ref[:, lanes].astype(jnp.float32)
        gamma = gam_ref[:, lanes].astype(jnp.float32)
        for p in range(pillars):
            weight = jnp.maximum(0.0, 1.0 - jnp.abs(node_iota - pos[p : p + 1, :]))
            grid[p * BIN : (p + 1) * BIN, lanes] = (delta[p : p + 1, :] * weight).astype(jnp.bfloat16)
            grid[nodes + p * BIN : nodes + (p + 1) * BIN, lanes] = (
                gamma[p : p + 1, :] * weight
            ).astype(jnp.bfloat16)
        return carry

    lax.fori_loop(0, trades // CHUNK, build, 0)

    def receive(turn):
        half = lax.rem(side + turn, 2)
        if turn == 0:
            for off in range(1, n):
                slot = lax.rem(me + n - off, n)
                gather_copy(slot, slot).wait_recv()
            swap_copy(half).start()
        else:
            swap_copy(half).wait_recv()
        line = jnp.concatenate([held[half, k, :rows, :] for k in range(n)], axis=1)
        curve = jnp.concatenate([held[half, k, rows:, :] for k in range(n)], axis=1)
        for h in range(H):
            live = (class_ref[...] >= h).astype(jnp.float32).astype(jnp.bfloat16)
            table[turn, h * rows : (h + 1) * rows, :nodes] = line * live
            table[turn, h * rows : (h + 1) * rows, nodes:] = curve * live

    total[...] = jnp.zeros_like(total)

    def respond(half, c, into, part):
        lanes = pl.ds(pl.multiple_of(c * CHUNK + part * SUB, SUB), SUB)
        into[:, part * SUB : (part + 1) * SUB] = jnp.dot(
            table[half], grid[:, lanes], preferred_element_type=jnp.float32
        )

    def settle(half, c, held_response, part):
        lanes = pl.ds(pl.multiple_of(c * CHUNK + part * SUB, SUB), SUB)
        growth = jnp.exp(held_response[:, part * SUB : (part + 1) * SUB]) - 1.0
        total[half] += lax.dot_general(
            owner[:, lanes],
            growth.astype(jnp.bfloat16),
            (((1,), (1,)), ((), ())),
            preferred_element_type=jnp.float32,
        )

    parts_of_chunk = CHUNK // SUB
    chunks = trades // CHUNK

    def advance(half, c, old, new):
        for part in range(parts_of_chunk):
            respond(half, c + 1, new, part)
            settle(half, c, old, part)

    def sweep(half):
        def pair(i, carry):
            advance(half, 2 * i, even, odd)
            advance(half, 2 * i + 1, odd, even)
            return carry

        lax.fori_loop(0, chunks // 2 - 1, pair, 0)
        advance(half, chunks - 2, even, odd)

    receive(0)
    for part in range(parts_of_chunk):
        respond(0, 0, even, part)
    sweep(0)
    receive(1)
    for part in range(parts_of_chunk):
        respond(1, 0, even, part)
        settle(0, chunks - 1, odd, part)
    sweep(1)
    for part in range(parts_of_chunk):
        settle(1, chunks - 1, odd, part)

    for k in range(n):
        for d in range(per_device):
            for h in range(H):
                row = k * per_device + d
                parts[k, d, h : h + 1, :] = jnp.concatenate(
                    [total[lax.rem(side + half, 2), row : row + 1, h * rows : (h + 1) * rows] for half in range(2)],
                    axis=1,
                )

    def share_copy(slot, peer):
        return pltpu.make_async_remote_copy(
            src_ref=parts.at[peer],
            dst_ref=landed.at[slot],
            send_sem=send_b.at[peer],
            recv_sem=recv_b.at[slot],
            device_id={"trade": peer},
            device_id_type=MESH,
        )

    for off in range(1, n):
        share_copy(me, lax.rem(me + off, n)).start()
    result = parts[me]
    for off in range(1, n):
        slot = lax.rem(me + n - off, n)
        share_copy(slot, slot).wait_recv()
        result = result + landed[slot]
    out_ref[...] = result[:, :H, :]
    for off in range(1, n):
        peer = lax.rem(me + off, n)
        gather_copy(me, peer).wait_send()
        share_copy(me, peer).wait_send()
    swap_copy(side).wait_send()


def body(shocks, node_class, positions, deltas, gammas, notional, block_desk):
    n = lax.axis_size("trade")
    scens, cols = shocks.shape
    pillars, trades = positions.shape
    nodes = n * cols
    per_device = 2
    desk_rows = -(-(per_device * n) // 16) * 16
    hbm = pl.BlockSpec(memory_space=pltpu.HBM)
    vmem = pl.BlockSpec(memory_space=pltpu.VMEM)
    return pl.pallas_call(
        functools.partial(kernel, n),
        out_shape=jax.ShapeDtypeStruct((per_device, H, scens), jnp.float32),
        in_specs=[hbm, vmem, hbm, hbm, hbm, hbm, pl.BlockSpec(memory_space=pltpu.SMEM)],
        out_specs=vmem,
        scratch_shapes=[
            pltpu.VMEM((scens, cols), jnp.float32),
            pltpu.VMEM((pillars, trades), jnp.bfloat16),
            pltpu.VMEM((pillars, trades), jnp.bfloat16),
            pltpu.VMEM((pillars, trades), jnp.bfloat16),
            pltpu.VMEM((trades,), jnp.bfloat16),
            pltpu.SemaphoreType.DMA((5,)),
            pltpu.VMEM((2, n, scens, cols), jnp.bfloat16),
            pltpu.VMEM((2, H * scens // 2, 2 * nodes), jnp.bfloat16),
            pltpu.VMEM((2 * nodes, trades), jnp.bfloat16),
            pltpu.VMEM((desk_rows, trades), jnp.bfloat16),
            pltpu.VMEM((2, desk_rows, H * scens // 2), jnp.float32),
            pltpu.VMEM((H * scens // 2, CHUNK), jnp.float32),
            pltpu.VMEM((H * scens // 2, CHUNK), jnp.float32),
            pltpu.VMEM((n, per_device, 8, scens), jnp.float32),
            pltpu.VMEM((n, per_device, 8, scens), jnp.float32),
            pltpu.SemaphoreType.DMA((n,)),
            pltpu.SemaphoreType.DMA((n,)),
            pltpu.SemaphoreType.DMA((n,)),
            pltpu.SemaphoreType.DMA((n,)),
            pltpu.SemaphoreType.DMA((2,)),
        ],
        compiler_params=pltpu.CompilerParams(
            collective_id=0, has_side_effects=True, vmem_limit_bytes=VLIM * 1024 * 1024
        ),
    )(
        shocks,
        node_class.reshape(1, -1),
        positions,
        deltas,
        gammas,
        notional,
        block_desk,
    )


def solution(mesh):
    in_specs = (
        P(("scen", "hz"), "trade"),
        P(),
        P(None, ("groups", "trade")),
        P(None, ("groups", "trade")),
        P(None, ("groups", "trade")),
        P(("groups", "trade")),
        P(("groups", "trade")),
    )
    out_specs = P(("groups", "trade"), None, ("scen", "hz"))
    return jax.shard_map(body, mesh=mesh, in_specs=in_specs, out_specs=out_specs, check_vma=False)
```

time: 30 us -> 24.5 us (0.82)
  local copies, waits for them, and re-layouts: 4.88 us -> 1.29 us
  Pallas kernels: 24.8 us -> 22.9 us
    unnamed x12 -> x0, local copies, waits for them, and re-layouts: 3.55 us -> none
    pallas_call x1, Pallas kernels: 24.8 us -> 22.9 us  [body(): pl.pallas_call(functools.partial(kernel, n), out_shape=jax.ShapeDtypeStru...]
    reshape x1 -> x0, local copies, waits for them, and re-layouts: 0.73 us -> none  [body(): notional.reshape(1, -1)]
    pallas_call x1, local copies, waits for them, and re-layouts: 0.6 us -> 1.29 us  [body(): pl.pallas_call(functools.partial(kernel, n), out_shape=jax.ShapeDtypeStru...]
where the time goes in v2:
time: 24.5 us; the launch traced here: 24.2 us
  Pallas kernels  22.9 us (93%)
  local copies, waits for them, and re-layouts  1.29 us (5%)
    pallas_call x1, Pallas kernels, body(): pl.pallas_call(functools.partial(kernel, n), out_shape=jax.ShapeDtypeStru...  22.9 us
    pallas_call x1, local copies, waits for them, and re-layouts, body(): pl.pallas_call(functools.partial(kernel, n), out_shape=jax.ShapeDtypeStru...  1.29 us

profile of v2, /device:TPU:0, one launch (start us, length us, event | category | flops | bytes accessed | tf_op | source)
XLA Modules:
  0.0 24.2 jit_solution(1533959097853542303)
XLA Ops:
  0.0 22.9 %shard_map.73 = f32[2,5,128]{2,1,0:T(8,128)} custom-call(f32[128,128]{1,0:T(8,128)} %shocks_hbm.1, s32[1,512]{1,0:T(1,128)} %bitcast.1, bf16[16,4096]{1,0:T(8,128)(2,1)} %pos_hbm.1, bf16[16,4096]{1,0:T(8,128)(2,1)} %del_hbm.1, bf16[16,4096]{1,0:T(8,128)(2,1)} %gam_hbm.1, bf16[4096]{0:T(1024)(128)(2,1)} %val_hbm.1, s32[32]{0:T(128)} %desk_ref.1), custom_call_target="tpu_custom_call" | custom-call | tf_op jit(solution)/shard_map/pallas_call | solution.py:219
  23.0 1.3 %copy.8 = f32[2,5,128]{2,0,1:T(2,128)} copy(f32[2,5,128]{2,1,0:T(8,128)} %shard_map.73) | data formatting | bytes 10240 | tf_op jit(solution)/shard_map/pallas_call | solution.py:219
